TPU v7x, 128 devices: a whole 4x4x4 slice. The times are simulated.
128 devices in a mesh: dom: 32 (over y, z_hi, x), orb: 4 (over z_lo, core).
Axes of the slice: x: 4, y: 4, z: 4 (z_hi: 2, z_lo: 2; z = z_hi * 2 + z_lo), core: 2. Of those that a mesh axis runs over, the one named last changes fastest.
Arguments:
- orbitals: float32 [32, 384, 2048], P('orb', 'dom'), may hold values from -40 to 40, as said below
- potential: float32 [384, 2048], P('dom'), may hold values from -2 to 1
- subspace: bfloat16 [2048, 384, 2048], P('orb', 'dom'), may hold values from -0.0068359375 to 0.0068359375
Outputs:
- correlation: float32 [32, 2048], P('dom', 'orb')
- projected: float32 [32, 2048], P('dom', 'orb')
Inputs may be any that keep to these rules, and one draw needn't show every extreme that they name: orbitals of the block, real-valued.
All inputs are finite; a program needn't handle non-finite values.
Results may differ from a plain program's by a relative error of at most 0.0021.
The roundings to bfloat16 on the way count: a program that leaves them out, or rounds other values in their place, can miss the bound.
Values may be sent and summed in bfloat16 or wider, within the bound.
A program may use at most 192 MiB of HBM per device.

v0:
```python
import jax
import jax.numpy as jnp
from jax import lax
from jax.sharding import PartitionSpec as P

NZ = 64


coeffs = (
    -5369.0 / 1800.0,
    12.0 / 7.0,
    -15.0 / 56.0,
    10.0 / 189.0,
    -1.0 / 112.0,
    2.0 / 1925.0,
    -1.0 / 16632.0,
)


def extended(cells, sides, width):
    for axis, dim in sides:
        count = lax.axis_size(axis)
        head = lax.slice_in_dim(cells, 0, width, axis=dim)
        tail = lax.slice_in_dim(cells, cells.shape[dim] - width, cells.shape[dim], axis=dim)
        cells = jnp.concatenate(
            [
                lax.ppermute(tail, axis, [(i, (i + 1) % count) for i in range(count)]),
                cells,
                lax.ppermute(head, axis, [((i + 1) % count, i) for i in range(count)]),
            ],
            axis=dim,
        )
    return cells


def hamiltonian(padded, potential):
    length = padded.shape[1] - 12
    center = padded[:, 6 : 6 + length]
    depth = center.shape[2]
    zpos = (jnp.arange(depth, dtype=jnp.int32) % NZ)[None, None, :]
    total = 3.0 * coeffs[0] * center
    for shift_k in range(1, 7):
        along = (
            padded[:, 6 + shift_k : 6 + shift_k + length]
            + padded[:, 6 - shift_k : 6 - shift_k + length]
        )
        along = along + jnp.roll(center, shift_k * NZ, 2) + jnp.roll(center, -shift_k * NZ, 2)
        lower = jnp.where(
            zpos >= shift_k, jnp.roll(center, shift_k, 2), jnp.roll(center, shift_k - NZ, 2)
        )
        upper = jnp.where(
            zpos < NZ - shift_k, jnp.roll(center, -shift_k, 2), jnp.roll(center, NZ - shift_k, 2)
        )
        along = along + lower + upper
        total = total + coeffs[shift_k] * along
    return -0.5 * total + potential[None] * center


def widened(field):
    return extended(field, (("dom", 1),), 6)


def shards(orbitals, potential, subspace):
    count = orbitals.shape[0]
    first = (hamiltonian(widened(orbitals), potential) - 8.0 * orbitals) / 8.0
    second = 2.0 * (hamiltonian(widened(first), potential) - 8.0 * first) / 8.0 - orbitals
    final_pad = extended(second, (("dom", 1),), 6)
    applied = hamiltonian(final_pad, potential).astype(jnp.bfloat16).reshape(count, -1)
    filtered = second.astype(jnp.bfloat16).reshape(count, -1)
    both = jnp.stack([filtered, applied], axis=0)
    flat_sub = subspace.reshape(subspace.shape[0], -1)
    all_cells = flat_sub.shape[1] * lax.axis_size("dom")
    own_sq = jnp.sum(jnp.square(filtered.astype(jnp.float32)), axis=1)
    total_rows = count * lax.axis_size("orb")
    placed = lax.dynamic_update_slice(
        jnp.zeros((total_rows,), jnp.float32), own_sq, (lax.axis_index("orb") * count,)
    )
    total_sq = lax.psum(placed, ("dom", "orb"))
    partial_gram = jnp.einsum(
        "arc,jc->arj",
        lax.all_gather(both, "orb", axis=1, tiled=True),
        flat_sub,
        preferred_element_type=jnp.float32,
    )
    gram = lax.psum_scatter(partial_gram, "dom", scatter_dimension=1, tiled=True)
    kept = gram.shape[1]
    mine = lax.dynamic_slice_in_dim(total_sq, lax.axis_index("dom") * kept, kept)
    scale = jnp.sqrt(mine / all_cells + 1e-06)
    return (gram[0] / scale[:, None], gram[1] / scale[:, None])


def solution(mesh):
    placed = (P("orb", "dom", None), P("dom", None), P("orb", "dom", None))
    return jax.shard_map(
        shards,
        mesh=mesh,
        in_specs=placed,
        out_specs=(P("dom", "orb"), P("dom", "orb")),
        check_vma=False,
    )
```

profile of v0, /device:TPU:0, one launch (start us, length us, event | category | flops | bytes accessed | tf_op | source)
XLA Modules:
  0.0 563.3 jit_solution(5314013361031064272)
XLA Ops:
  8.5 1.6 collective-permute-start.1
  10.1 7.1 %collective-permute-start = (f32[8,6,2048]{2,0,1:T(8,128)S(1)}, f32[8,6,2048]{2,0,1:T(8,128)S(1)}, u32[]{:S(2)}, u32[]{:S(2)}) collective-permute-start(f32[8,6,2048]{2,0,1:T(8,128)S(1)} %get-tuple-element.215), channel_id=1, source_target_pairs={{4,0},{8,4},{12,8},{16,12},{20,16},{24,20},{28,24},{32,28},{36,32}... | collective-permute-start | bytes 1179656 | tf_op jit(solution)/shard_map/ppermute | solution.py:29
  41.1 9.2 %broadcast_multiply_fusion = (f32[8,12,2048]{2,0,1:T(8,128)S(1)}, f32[8,12,2048]{2,0,1:T(8,128)}) fusion(f32[8,12,2048]{2,0,1:T(8,128)S(1)} %copy-done, f32[12,2048]{1,0:T(8,128)S(1)} %copy-done.1, f32[8,12,1990]{2,0,1:T(8,128)S(1)} %get-tuple-element.228, f32[8,12,58]{2,0,1:T(8,128)} %get-tuple-element.230, f32[8,12,6]{2,0,1:T(8,128)} %get-tuple-element.224, ...), kind=kLoop, calls=%fused_computation.239 | loop fusion | flops 19070976 | bytes 40230912 | tf_op jit(solution)/shard_map/div | solution.py:65
  54.3 1.5 fusion.223
  58.5 1.5 fusion.234
  60.0 1.4 fusion.235
  67.2 1.5 fusion.211
  86.5 1.9 collective-permute-start.2
  89.7 7.4 %collective-permute-done.2 = f32[8,6,2048]{2,0,1:T(8,128)S(1)} collective-permute-done((f32[8,6,2048]{2,0,1:T(8,128)S(1)}, f32[8,6,2048]{2,0,1:T(8,128)S(1)}, u32[]{:S(2)}, u32[]{:S(2)}) %collective-permute-start.2) | collective-permute-done | bytes 393248 | tf_op jit(solution)/shard_map/ppermute | solution.py:29
  97.1 7.1 %collective-permute-done.3 = f32[8,6,2048]{2,0,1:T(8,128)S(1)} collective-permute-done((f32[8,6,2048]{2,0,1:T(8,128)S(1)}, f32[8,6,2048]{2,0,1:T(8,128)S(1)}, u32[]{:S(2)}, u32[]{:S(2)}) %collective-permute-start.3) | collective-permute-done | bytes 393248 | tf_op jit(solution)/shard_map/ppermute | solution.py:27
  105.0 15.1 %multiply_reduce_fusion = (f32[8]{0:T(128)}, bf16[8,12,2048]{2,0,1:T(8,128)(2,1)S(1)}, f32[8,12,2048]{2,0,1:T(8,128)S(1)}) fusion(f32[8,12,2048]{2,0,1:T(8,128)S(1)} %copy-done, f32[8,12,2048]{2,0,1:T(8,128)} %get-tuple-element.6, f32[12,2048]{1,0:T(8,128)} %broadcast_multiply_fusion.1, f32[8,12,1990]{2,0,1:T(8,128)} %get-tuple-element.152, ...), kind=kLoop, calls=%fused_computation.237 | loop fusion | flops 22216696 | bytes 32759840 | tf_op jit(solution)/shard_map/reduce_sum | solution.py:73
  121.6 1.5 fusion.174
  130.1 1.5 fusion.192
  133.0 1.5 fusion.198
  155.5 1.6 collective-permute-start.5
  158.2 6.1 %collective-permute-done.4 = f32[8,6,2048]{2,0,1:T(8,128)} collective-permute-done((f32[8,6,2048]{2,0,1:T(8,128)S(1)}, f32[8,6,2048]{2,0,1:T(8,128)}, u32[]{:S(2)}, u32[]{:S(2)}) %collective-permute-start.4) | collective-permute-done | bytes 393248 | tf_op jit(solution)/shard_map/ppermute | solution.py:29
  164.3 6.2 %collective-permute-done.5 = f32[8,6,2048]{2,0,1:T(8,128)} collective-permute-done((f32[8,6,2048]{2,0,1:T(8,128)S(1)}, f32[8,6,2048]{2,0,1:T(8,128)}, u32[]{:S(2)}, u32[]{:S(2)}) %collective-permute-start.5) | collective-permute-done | bytes 393248 | tf_op jit(solution)/shard_map/ppermute | solution.py:27
  170.4 14.3 %fusion.150 = bf16[8,12,2048]{2,0,1:T(8,128)(2,1)} fusion(f32[8,12,2048]{2,0,1:T(8,128)S(1)} %get-tuple-element.4, f32[8,12,1990]{2,0,1:T(8,128)} %get-tuple-element.78, f32[8,12,58]{2,0,1:T(8,128)} %get-tuple-element.80, f32[8,12,6]{2,0,1:T(8,128)} %get-tuple-element.74, f32[8,12,2042]{2,0,1:T(8,128)} %get-tuple-element.76, ...), kind=kLoop, calls=%fused_computation.238 | loop fusion | flops 21037056 | bytes 30400512 | tf_op jit(solution)/shard_map/convert_element_type | solution.py:68
  184.7 2.0 pad_maximum_fusion.4
  186.7 32.8 %copy.7 = bf16[512,12,2048]{0,2,1:T(8,128)(2,1)} copy(bf16[512,12,2048]{2,0,1:T(8,128)(2,1)} %param.5) | data formatting | bytes 50331648 | tf_op args[2]
  219.5 11.2 %fusion.281 = f32[2,32,512]{2,1,0:T(8,128)S(1)} fusion(bf16[2,32,24576]{2,1,0:T(8,128)(2,1)} %all-gather.2.cloned.1.call-done, bf16[512,24576,1]{0,1,2:T(8,128)(2,1)} %bitcast.13), kind=kOutput, calls=%fused_computation.377 | convolution fusion | flops 1610612736 | bytes 28442624 | tf_op jit(solution)/shard_map/arc,jc->arj/dot_general | solution.py:79
  232.4 66.5 %psum.7 = f32[32]{0:T(128)S(1)} all-reduce(f32[32]{0:T(128)S(1)} %dynamic_update_slice.3), channel_id=1, replica_groups=mesh['dom'=32,'orb'=4] {'dom','orb'}, use_global_device_ids=true, to_apply=%region_2.3 | all-reduce | flops 32 | bytes 256 | tf_op jit(solution)/shard_map/psum | solution.py:78
  300.3 254.2 %all-reduce.3.cloned.1.call-done = f32[2,32,512]{2,0,1:T(2,128)} async-done(((f32[2,32,512]{2,0,1:T(2,128)}), f32[2,32,512]{2,0,1:T(2,128)}) %all-reduce.3.cloned.1.call-update) | async-done | bytes 131088
  554.5 2.0 fusion.167
  (148 shorter events, 91.8 us)
Async XLA Ops:
  7.2 11.3 %copy-start = (f32[8,12,2048]{2,0,1:T(8,128)S(1)}, f32[8,12,2048]{2,0,1:T(8,128)}, u32[]{:S(2)}) copy-start(f32[8,12,2048]{2,0,1:T(8,128)} %param.3) | copy-start | bytes 2359300
  7.2 212.4 %all-gather.2.cloned.1.call-start = ((), (), s32[]{:S(2)}) async-start(), calls=%async_computation | async-start | bytes 3932160 | tf_op jit(solution)/shard_map/all_gather | solution.py:81
  8.5 32.4 %collective-permute-start.1 = (f32[8,6,2048]{2,0,1:T(8,128)S(1)}, f32[8,6,2048]{2,0,1:T(8,128)S(1)}, u32[]{:S(2)}, u32[]{:S(2)}) collective-permute-start(f32[8,6,2048]{2,0,1:T(8,128)S(1)} %get-tuple-element.216), channel_id=1, source_target_pairs={{0,4},{4,8},{8,12},{12,16},{16,20},{20,24},{24,28},{28,32},{32,36}... | collective-permute-start | bytes 1179656 | tf_op jit(solution)/shard_map/ppermute | solution.py:27
  10.1 30.9 %collective-permute-start = (f32[8,6,2048]{2,0,1:T(8,128)S(1)}, f32[8,6,2048]{2,0,1:T(8,128)S(1)}, u32[]{:S(2)}, u32[]{:S(2)}) collective-permute-start(f32[8,6,2048]{2,0,1:T(8,128)S(1)} %get-tuple-element.215), channel_id=1, source_target_pairs={{4,0},{8,4},{12,8},{16,12},{20,16},{24,20},{28,24},{32,28},{36,32}... | collective-permute-start | bytes 1179656 | tf_op jit(solution)/shard_map/ppermute | solution.py:29
  17.2 23.8 %copy-start.4 = (pred[2048]{0:T(1024)(128)(4,1)}, pred[2048]{0:T(1024)(128)(4,1)S(1)}, u32[]{:S(2)}) copy-start(pred[2048]{0:T(1024)(128)(4,1)S(1)} %get-tuple-element.237) | copy-start | bytes 6148
  17.2 23.8 %copy-start.5 = (pred[2048]{0:T(1024)(128)(4,1)}, pred[2048]{0:T(1024)(128)(4,1)S(1)}, u32[]{:S(2)}) copy-start(pred[2048]{0:T(1024)(128)(4,1)S(1)} %get-tuple-element.238) | copy-start | bytes 6148
  17.3 23.8 %copy-start.6 = (pred[2048]{0:T(1024)(128)(4,1)}, pred[2048]{0:T(1024)(128)(4,1)S(1)}, u32[]{:S(2)}) copy-start(pred[2048]{0:T(1024)(128)(4,1)S(1)} %get-tuple-element.239) | copy-start | bytes 6148
  17.3 23.8 %copy-start.7 = (pred[2048]{0:T(1024)(128)(4,1)}, pred[2048]{0:T(1024)(128)(4,1)S(1)}, u32[]{:S(2)}) copy-start(pred[2048]{0:T(1024)(128)(4,1)S(1)} %get-tuple-element.240) | copy-start | bytes 6148
  31.8 8.3 %copy-start.1 = (f32[12,2048]{1,0:T(8,128)S(1)}, f32[12,2048]{1,0:T(8,128)}, u32[]{:S(2)}) copy-start(f32[12,2048]{1,0:T(8,128)} %param.4) | copy-start | bytes 294916
  86.5 10.6 %collective-permute-start.2 = (f32[8,6,2048]{2,0,1:T(8,128)S(1)}, f32[8,6,2048]{2,0,1:T(8,128)S(1)}, u32[]{:S(2)}, u32[]{:S(2)}) collective-permute-start(f32[8,6,2048]{2,0,1:T(8,128)S(1)} %get-tuple-element.141), channel_id=1, source_target_pairs={{4,0},{8,4},{12,8},{16,12},{20,16},{24,20},{28,24},{32,28},{36,32}... | collective-permute-start | bytes 1179656 | tf_op jit(solution)/shard_map/ppermute | solution.py:29
  88.5 15.7 %collective-permute-start.3 = (f32[8,6,2048]{2,0,1:T(8,128)S(1)}, f32[8,6,2048]{2,0,1:T(8,128)S(1)}, u32[]{:S(2)}, u32[]{:S(2)}) collective-permute-start(f32[8,6,2048]{2,0,1:T(8,128)S(1)} %get-tuple-element.142), channel_id=1, source_target_pairs={{0,4},{4,8},{8,12},{12,16},{16,20},{20,24},{24,28},{28,32},{32,36}... | collective-permute-start | bytes 1179656 | tf_op jit(solution)/shard_map/ppermute | solution.py:27
  97.1 7.1 %copy-start.2 = (f32[8,6,2048]{2,0,1:T(8,128)}, f32[8,6,2048]{2,0,1:T(8,128)S(1)}, u32[]{:S(2)}) copy-start(f32[8,6,2048]{2,0,1:T(8,128)S(1)} %collective-permute-done.2) | copy-start | bytes 1179652
  104.2 0.8 copy-start.3
  155.1 9.2 %collective-permute-start.4 = (f32[8,6,2048]{2,0,1:T(8,128)S(1)}, f32[8,6,2048]{2,0,1:T(8,128)}, u32[]{:S(2)}, u32[]{:S(2)}) collective-permute-start(f32[8,6,2048]{2,0,1:T(8,128)S(1)} %get-tuple-element.67), channel_id=1, source_target_pairs={{4,0},{8,4},{12,8},{16,12},{20,16},{24,20},{28,24},{32,28},{36,32}... | collective-permute-start | bytes 1179656 | tf_op jit(solution)/shard_map/ppermute | solution.py:29
  155.5 14.9 %collective-permute-start.5 = (f32[8,6,2048]{2,0,1:T(8,128)S(1)}, f32[8,6,2048]{2,0,1:T(8,128)}, u32[]{:S(2)}, u32[]{:S(2)}) collective-permute-start(f32[8,6,2048]{2,0,1:T(8,128)S(1)} %get-tuple-element.68), channel_id=1, source_target_pairs={{0,4},{4,8},{8,12},{12,16},{16,20},{20,24},{24,28},{28,32},{32,36}... | collective-permute-start | bytes 1179656 | tf_op jit(solution)/shard_map/ppermute | solution.py:27
  186.7 367.8 %all-reduce.3.cloned.1.call-start = ((), (), s32[]{:S(2)}) async-start(), calls=%async_computation.1 | async-start | bytes 262144
  219.5 12.1 %copy-start.8 = (f32[8]{0:T(128)S(1)}, f32[8]{0:T(128)}, u32[]{:S(2)}) copy-start(f32[8]{0:T(128)} %get-tuple-element.2) | copy-start | bytes 100
  219.5 12.3 %copy-start.9 = (u32[128]{0:T(128)S(1)}, u32[128]{0:T(128)}, u32[]{:S(2)}) copy-start(u32[128]{0:T(128)} %constant.99) | copy-start | bytes 1540
Sparse Core Ops, SparseCore 0:
  186.8 31.7 all-gather.1
  231.7 322.7 all-reduce.2
where the time goes:
time: 564 us; the launch traced here: 563 us
  waiting for transfers between devices  281 us (50%)
  local copies, waits for them, and re-layouts  132 us (23%)
  blocking collectives  66.5 us (12%)
  other arithmetic  44.3 us (8%)
  between operations  15 us (3%)
  starting transfers between devices  12.9 us (2%)
  matrix products  11.2 us (2%)
    unnamed x3, waiting for transfers between devices  254 us
    psum x1, blocking collectives, shards(): total_sq = lax.psum(placed, ('dom', 'orb'))  66.5 us
    unnamed x24, local copies, waits for them, and re-layouts  34.4 us
    slice x36, local copies, waits for them, and re-layouts, hamiltonian(): jnp.roll(center, shift_k * NZ, 2)  32.7 us
    slice x36, local copies, waits for them, and re-layouts, hamiltonian(): jnp.roll(center, shift_k - NZ, 2)  31.5 us
    slice x36, local copies, waits for them, and re-layouts, hamiltonian(): jnp.roll(center, shift_k, 2)  30.8 us
    reduce_sum x1, other arithmetic, shards(): own_sq = jnp.sum(jnp.square(filtered.astype(jnp.float32)), axis=1)  15.1 us
    convert_element_type x1, other arithmetic, shards(): hamiltonian(final_pad, potential).astype(jnp.bfloat16).reshape(count, -1)  14.3 us
  transfers between devices with their start and end apart: 8, of which 5 were waited for; matrix products, arithmetic and copies ran while one was open for 11% of the time, Pallas kernels for 0%

commit v1 on v0

v1 whole, which is shorter than its diff:
```python
import jax
import jax.numpy as jnp
from jax import lax
from jax.experimental import pallas as pl
from jax.experimental.pallas import tpu as pltpu
from jax.sharding import PartitionSpec as P

BF = jnp.bfloat16
F32 = jnp.float32
MESH = pl.DeviceIdType.MESH

coeffs = (
    -5369.0 / 1800.0,
    12.0 / 7.0,
    -15.0 / 56.0,
    10.0 / 189.0,
    -1.0 / 112.0,
    2.0 / 1925.0,
    -1.0 / 16632.0,
)
A = [-0.5 * c for c in coeffs]

NZ = 64
PLANE = 2048
EXT = 384
GROUP = 4
DOM = 32
CELLS = 786432


def z_matrix():
    row = lax.broadcasted_iota(jnp.int32, (128, 128), 0)
    col = lax.broadcasted_iota(jnp.int32, (128, 128), 1)
    same = (row >= NZ) == (col >= NZ)
    apart = (row - col) & (NZ - 1)
    m = jnp.zeros((128, 128), F32)
    for k in range(1, 7):
        m = jnp.where(same & ((apart == k) | (apart == NZ - k)), A[k], m)
    hi = m.astype(BF)
    lo = (m - hi.astype(F32)).astype(BF)
    top = jnp.concatenate([hi, lo], axis=1)
    low = jnp.concatenate([hi, jnp.zeros_like(hi)], axis=1)
    return jnp.concatenate([top, low], axis=0)


def hamiltonian(src, planes, pots, w, ext):
    xs = [src[i] for i in planes]
    lhs = []
    for x in xs:
        t = jnp.concatenate([x[:, c * 128 : (c + 1) * 128] for c in range(16)], axis=0)
        hi = t.astype(BF)
        lo = (t - hi.astype(F32)).astype(BF)
        lhs.append(jnp.concatenate([hi, lo], axis=1))
    z = jnp.dot(jnp.concatenate(lhs, axis=0), w[...], preferred_element_type=F32)
    z = z[:, :128] + z[:, 128:]
    outs = []
    for j, (i, x) in enumerate(zip(planes, xs)):
        turned = pltpu.roll(x, NZ, 1)
        for e, v in ((0, x), (1, turned)):
            ext[j, e, :, EXT : EXT + PLANE] = v
            ext[j, e, :, :EXT] = v[:, PLANE - EXT :]
            ext[j, e, :, EXT + PLANE :] = v[:, :EXT]

        def along_y(k):
            odd = k % 2
            start = EXT + NZ * (k + odd)
            return ext[j, odd, :, start : start + PLANE]

        acc = (3 * A[0] + pots[j]) * x
        acc = acc + jnp.concatenate(
            [z[j * 128 + c * 8 : j * 128 + c * 8 + 8] for c in range(16)], axis=1
        )
        for k in range(1, 7):
            acc = acc + A[k] * (
                (src[i + k] + src[i - k]) + (along_y(k) + along_y(-k))
            )
        outs.append(acc)
    return xs, outs


def kernel(
    orb_hbm, pot, sub_hbm, corr, proj,
    orbs, own16, left16, right16, first, second, fleft, fright, rows16, pots, ext, w,
    sub, even, odd, squares, msg, got,
    s_loc, s_sub, s_toright, s_toleft, r_left, r_right, s_pot, r_pot,
    s_fright, s_fleft, r_fleft, r_fright,
    s_z, r_z, s_c, r_c, s_f, r_f, s_all, r_all,
):
    d = lax.axis_index("dom")
    b = lax.axis_index("orb")
    right = (lax.rem(d + 1, DOM), b)
    left = (lax.rem(d + DOM - 1, DOM), b)
    b_z = lax.rem(b + 2, 4)
    b_c = b + 1 - 2 * lax.rem(b, 2)
    b_zc = lax.rem(b_c + 2, 4)

    barrier = pltpu.get_barrier_semaphore()

    def greet(k, carry):
        pl.semaphore_signal(
            barrier, inc=1, device_id=(lax.rem(d + k, DOM), b), device_id_type=MESH
        )
        return carry

    lax.fori_loop(1, DOM, greet, 0)
    for peer in (b_z, b_c, b_zc):
        pl.semaphore_signal(barrier, inc=1, device_id=(d, peer), device_id_type=MESH)

    load = pltpu.make_async_copy(orb_hbm, orbs.at[pl.ds(12, 12)], s_loc)
    load.start()

    def load_sub(p):
        return pltpu.make_async_copy(sub_hbm.at[p], sub.at[p], s_sub.at[p])

    def start_sub(p, carry):
        load_sub(p).start()
        return carry

    lax.fori_loop(0, 12, start_sub, 0)
    w[...] = z_matrix()
    for p in range(12):
        pots[6 + p] = pot[p : p + 1, :]
    load.wait()

    def narrow(q, carry):
        own16[q] = jnp.concatenate([orbs[12 + 2 * q], orbs[13 + 2 * q]], axis=0).astype(BF)
        return carry

    lax.fori_loop(0, 6, narrow, 0)

    def remote(src, dst, ss, rs, device):
        return pltpu.make_async_remote_copy(
            src_ref=src, dst_ref=dst, send_sem=ss, recv_sem=rs,
            device_id=device, device_id_type=MESH,
        )

    def orb_right(q):
        return remote(own16.at[q], left16.at[q], s_toright.at[q], r_left.at[q], right)

    def orb_left(q):
        return remote(own16.at[q], right16.at[q], s_toleft.at[q], r_right.at[q], left)

    pot_right = remote(
        pots.at[pl.ds(12, 6)], pots.at[pl.ds(0, 6)], s_pot.at[0], r_pot.at[0], right
    )
    pot_left = remote(
        pots.at[pl.ds(6, 6)], pots.at[pl.ds(18, 6)], s_pot.at[1], r_pot.at[1], left
    )

    pl.semaphore_wait(barrier, DOM - 1 + 3)

    def send_orbs(j, carry):
        orb_right(5 - j).start()
        orb_left(j).start()
        return carry

    lax.fori_loop(0, 3, send_orbs, 0)
    pot_right.start()
    pot_left.start()
    lax.fori_loop(3, 6, send_orbs, 0)

    def widen(src, q, dst, at):
        both = src[q].astype(F32)
        dst[at] = both[:8]
        dst[at + 1] = both[8:]

    def take_orbs(j, carry):
        orb_right(5 - j).wait_recv()
        widen(left16, 5 - j, orbs, 2 * (5 - j))
        orb_left(j).wait_recv()
        widen(right16, j, orbs, 24 + 2 * j)
        return carry

    lax.fori_loop(0, 3, take_orbs, 0)

    def first_of(planes):
        xs, hs = hamiltonian(
            orbs, [p + 12 for p in planes], [pots[p + 6] for p in planes], w, ext
        )
        for p, x, h in zip(planes, xs, hs):
            first[p + 6] = 0.125 * h - x

    def inner(g, carry):
        first_of([g * GROUP + j for j in range(GROUP)])
        return carry

    lax.fori_loop(0, 3, inner, 0)
    pot_right.wait_recv()
    pot_left.wait_recv()

    def to_z(a, q):
        n = a * 6 + q
        return remote(
            rows16.at[a, b, q], rows16.at[a, b, q], s_z.at[n], r_z.at[n], (d, b_z)
        )

    def to_c(a, q):
        n = a * 6 + q
        return remote(
            rows16.at[a, b, q], rows16.at[a, b, q], s_c.at[n], r_c.at[n], (d, b_c)
        )

    def forward(a, q):
        n = a * 6 + q
        return remote(
            rows16.at[a, b_z, q], rows16.at[a, b_z, q], s_f.at[n], r_f.at[n], (d, b_c)
        )

    def come_z(a, q):
        n = a * 6 + q
        return remote(
            rows16.at[a, b_z, q], rows16.at[a, b_z, q], s_z.at[n], r_z.at[n], (d, b_z)
        )

    def come_c(a, q):
        n = a * 6 + q
        return remote(
            rows16.at[a, b_c, q], rows16.at[a, b_c, q], s_c.at[n], r_c.at[n], (d, b_c)
        )

    def come_f(a, q):
        n = a * 6 + q
        return remote(
            rows16.at[a, b_zc, q], rows16.at[a, b_zc, q], s_f.at[n], r_f.at[n], (d, b_c)
        )

    def filt_right(j):
        return remote(
            rows16.at[0, b, 3 + j], fleft.at[j], s_fright.at[j], r_fleft.at[j], right
        )

    def filt_left(j):
        return remote(
            rows16.at[0, b, j], fright.at[j], s_fleft.at[j], r_fright.at[j], left
        )

    def outer(s, carry):
        take_orbs(3 + s, 0)
        first_of([-2 - 2 * s, -1 - 2 * s, 12 + 2 * s, 13 + 2 * s])
        planes = [4 - 2 * s, 5 - 2 * s, 6 + 2 * s, 7 + 2 * s]
        xs, hs = hamiltonian(
            first, [p + 6 for p in planes], [pots[p + 6] for p in planes], w, ext
        )
        out = []
        for p, x, h in zip(planes, xs, hs):
            v = 0.25 * h - 2.0 * x - orbs[p + 12]
            second[p + 6] = v
            out.append(v)
        rows16[0, b, 2 - s] = jnp.concatenate(out[:2], axis=0).astype(BF)
        rows16[0, b, 3 + s] = jnp.concatenate(out[2:], axis=0).astype(BF)
        filt_left(2 - s).start()
        filt_right(s).start()
        to_z(0, 2 - s).start()
        to_z(0, 3 + s).start()
        to_c(0, 2 - s).start()
        to_c(0, 3 + s).start()
        return carry

    lax.fori_loop(0, 3, outer, 0)

    def pass_on(s, carry):
        come_z(0, 2 - s).wait_recv()
        forward(0, 2 - s).start()
        come_z(0, 3 + s).wait_recv()
        forward(0, 3 + s).start()
        return carry

    lax.fori_loop(0, 2, pass_on, 0)

    def take_filt(j, carry):
        filt_right(j).wait_recv()
        widen(fleft, j, second, 2 * j)
        filt_left(2 - j).wait_recv()
        widen(fright, 2 - j, second, 18 + 2 * (2 - j))
        return carry

    lax.fori_loop(0, 3, take_filt, 0)

    def last(g, carry):
        planes = [g * GROUP + j for j in range(GROUP)]
        _, hs = hamiltonian(
            second, [p + 6 for p in planes], [pots[p + 6] for p in planes], w, ext
        )
        rows16[1, b, 2 * g] = jnp.concatenate(hs[:2], axis=0).astype(BF)
        rows16[1, b, 2 * g + 1] = jnp.concatenate(hs[2:], axis=0).astype(BF)
        for q in (2 * g, 2 * g + 1):
            to_z(1, q).start()
            to_c(1, q).start()
        return carry

    lax.fori_loop(0, 3, last, 0)
    pass_on(2, 0)

    even[...] = jnp.zeros_like(even)
    odd[...] = jnp.zeros_like(odd)
    squares[...] = jnp.zeros_like(squares)

    def come_on(q):
        come_z(1, q).wait_recv()
        forward(1, q).start()

    def gram(q):
        for a in range(2):
            come_c(a, q).wait_recv()
            come_f(a, q).wait_recv()
        load_sub(2 * q).wait()
        load_sub(2 * q + 1).wait()
        filt = jnp.concatenate([rows16[0, o, q] for o in range(4)], axis=0)
        appl = jnp.concatenate([rows16[1, o, q] for o in range(4)], axis=0)
        rows = jnp.concatenate([filt, appl], axis=0)
        nt = (((1,), (1,)), ((), ()))
        even[...] += lax.dot_general(sub[2 * q], rows, nt, preferred_element_type=F32)
        odd[...] += lax.dot_general(sub[2 * q + 1], rows, nt, preferred_element_type=F32)
        total = squares[...]
        for c in range(16):
            x = filt[:, c * 128 : (c + 1) * 128].astype(F32)
            total = total + x * x
        squares[...] = total

    come_on(0)

    def step(q, carry):
        come_on(q + 1)
        gram(q)
        return carry

    lax.fori_loop(0, 5, step, 0)
    gram(5)

    from_even = even[...].T
    from_odd = odd[...].T
    sq = squares[...]
    for o in range(4):
        for a in range(2):
            at = a * 64 + o * 16
            block = from_even[at : at + 8] + from_odd[at + 8 : at + 16]
            for c in range(4):
                msg[pl.ds(o * 128 + a * 4 + c, 8, stride=16), :] = block[
                    :, c * 128 : (c + 1) * 128
                ]
        msg[pl.ds(o * 128 + 8, 8, stride=16), :] = sq[o * 16 : o * 16 + 8] + sq[o * 16 + 8 : o * 16 + 16]

    def to_all(k):
        t = lax.rem(d + k, DOM)
        return remote(
            msg.at[pl.ds(t * 16, 16)], got.at[pl.ds(d * 16, 16)],
            s_all.at[k - 1], r_all.at[k - 1], (t, b),
        )

    def from_all(k):
        t = lax.rem(d + DOM - k, DOM)
        return remote(
            msg.at[pl.ds(t * 16, 16)], got.at[pl.ds(t * 16, 16)],
            s_all.at[k - 1], r_all.at[k - 1], (t, b),
        )

    def send_all(k, carry):
        to_all(k).start()
        return carry

    lax.fori_loop(1, DOM, send_all, 0)
    got[pl.ds(d * 16, 16), :] = msg[pl.ds(d * 16, 16), :]

    def wait_sends(j, carry):
        orb_right(j).wait_send()
        orb_left(j).wait_send()
        for a in range(2):
            to_z(a, j).wait_send()
            to_c(a, j).wait_send()
            forward(a, j).wait_send()
        return carry

    lax.fori_loop(0, 6, wait_sends, 0)

    def wait_filt(j, carry):
        filt_right(j).wait_send()
        filt_left(j).wait_send()
        return carry

    lax.fori_loop(0, 3, wait_filt, 0)
    pot_right.wait_send()
    pot_left.wait_send()

    def wait_all(k, carry):
        from_all(k).wait_recv()
        return carry

    lax.fori_loop(1, DOM, wait_all, 0)
    total = got[pl.ds(0, 16), :]
    for t in range(1, DOM):
        total = total + got[pl.ds(t * 16, 16), :]
    scale = jnp.sqrt(jnp.sum(total[8:9, :], axis=1, keepdims=True) / CELLS + 1e-06)
    total = total[:8] / scale
    for c in range(4):
        corr[:, c * 128 : (c + 1) * 128] = total[c : c + 1]
        proj[:, c * 128 : (c + 1) * 128] = total[4 + c : 5 + c]

    def wait_sent(k, carry):
        to_all(k).wait_send()
        return carry

    lax.fori_loop(1, DOM, wait_sent, 0)


def shards(orbitals, potential, subspace):
    dma = pltpu.SemaphoreType.DMA
    return pl.pallas_call(
        kernel,
        out_shape=[jax.ShapeDtypeStruct((1, 512), F32)] * 2,
        in_specs=[
            pl.BlockSpec(memory_space=pl.ANY),
            pl.BlockSpec(memory_space=pltpu.VMEM),
            pl.BlockSpec(memory_space=pl.ANY),
        ],
        out_specs=[pl.BlockSpec(memory_space=pltpu.VMEM)] * 2,
        scratch_shapes=[
            pltpu.VMEM((36, 8, PLANE), F32),
            pltpu.VMEM((6, 16, PLANE), BF),
            pltpu.VMEM((6, 16, PLANE), BF),
            pltpu.VMEM((6, 16, PLANE), BF),
            pltpu.VMEM((24, 8, PLANE), F32),
            pltpu.VMEM((24, 8, PLANE), F32),
            pltpu.VMEM((3, 16, PLANE), BF),
            pltpu.VMEM((3, 16, PLANE), BF),
            pltpu.VMEM((2, 4, 6, 16, PLANE), BF),
            pltpu.VMEM((24, 1, PLANE), F32),
            pltpu.VMEM((GROUP, 2, 8, PLANE + 2 * EXT), F32),
            pltpu.VMEM((256, 256), BF),
            pltpu.VMEM((12, 512, PLANE), BF),
            pltpu.VMEM((512, 128), F32),
            pltpu.VMEM((512, 128), F32),
            pltpu.VMEM((64, 128), F32),
            pltpu.VMEM((DOM * 16, 128), F32),
            pltpu.VMEM((DOM * 16, 128), F32),
            dma(()), dma((12,)),
            dma((6,)), dma((6,)), dma((6,)), dma((6,)), dma((2,)), dma((2,)),
            dma((3,)), dma((3,)), dma((3,)), dma((3,)),
            dma((12,)), dma((12,)), dma((12,)), dma((12,)), dma((12,)), dma((12,)),
            dma((DOM - 1,)), dma((DOM - 1,)),
        ],
        compiler_params=pltpu.CompilerParams(
            collective_id=0, has_side_effects=True, vmem_limit_bytes=48 * 2**20
        ),
    )(orbitals.transpose(1, 0, 2), potential, subspace.transpose(1, 0, 2))


def solution(mesh):
    placed = (P("orb", "dom", None), P("dom", None), P("orb", "dom", None))
    return jax.shard_map(
        shards,
        mesh=mesh,
        in_specs=placed,
        out_specs=(P("dom", "orb"), P("dom", "orb")),
        check_vma=False,
    )
```

time: 564 us -> 58.3 us (0.10)
  waiting for transfers between devices: 281 us -> 0 us
  local copies, waits for them, and re-layouts: 132 us -> 3.19 us
  blocking collectives: 66.5 us -> 0 us
  Pallas kernels: 0 us -> 54.2 us
  other arithmetic: 44.3 us -> 0 us
  between operations: 15 us -> 0.65 us
  starting transfers between devices: 12.9 us -> 0 us
  matrix products: 11.2 us -> 0 us
    unnamed x3 -> x0, waiting for transfers between devices: 254 us -> none
    slice x111 -> x0, local copies, waits for them, and re-layouts: 96.3 us -> none  [the longest x36 32.7 us: hamiltonian(): jnp.roll(center, shift_k * NZ, 2)]
    psum x1 -> x0, blocking collectives: 66.5 us -> none  [shards(): total_sq = lax.psum(placed, ('dom', 'orb'))]
    pallas_call x0 -> x1, Pallas kernels: none -> 54.2 us  [shards(): pl.pallas_call(kernel, out_shape=[jax.ShapeDtypeStruct((1, 512), F32)] *...]
    unnamed x24 -> x6, local copies, waits for them, and re-layouts: 34.4 us -> 3.19 us
    ppermute x6 -> x0, waiting for transfers between devices: 26.7 us -> none  [the longest x3 13.4 us: extended(): lax.ppermute(head, axis, [((i + 1) % count, i) for i in range(count)])]
    reduce_sum x1 -> x0, other arithmetic: 15.1 us -> none  [shards(): own_sq = jnp.sum(jnp.square(filtered.astype(jnp.float32)), axis=1)]
    convert_element_type x1 -> x0, other arithmetic: 14.3 us -> none  [shards(): hamiltonian(final_pad, potential).astype(jnp.bfloat16).reshape(count, -1)]
  transfers between devices with their start and end apart: 8 -> 0, of which waited for: 5 -> 0; matrix products, arithmetic and copies ran while one was open for 11% -> 0% of each run, Pallas kernels for 0% -> 0%
where the time goes in v1:
time: 58.3 us; the launch traced here: 58.1 us
  Pallas kernels  54.2 us (93%)
  local copies, waits for them, and re-layouts  3.19 us (5%)
  between operations  0.65 us (1%)
    pallas_call x1, Pallas kernels, shards(): pl.pallas_call(kernel, out_shape=[jax.ShapeDtypeStruct((1, 512), F32)] *...  54.2 us
    unnamed x6, local copies, waits for them, and re-layouts  3.19 us

profile of v1, /device:TPU:0, one launch (start us, length us, event | category | flops | bytes accessed | tf_op | source)
XLA Modules:
  0.0 58.1 jit_solution(2958903596364625988)
XLA Ops:
  0.6 0.0 copy-start
  0.6 1.1 %copy-done = f32[8,12,2048]{2,0,1:T(8,128)S(1)} copy-done((f32[8,12,2048]{2,0,1:T(8,128)S(1)}, f32[8,12,2048]{2,0,1:T(8,128)}, u32[]{:S(2)}) %copy-start) | copy-done | bytes 786456
  1.8 0.0 copy-start.1
  1.8 0.9 %copy-done.1 = f32[12,2048]{1,0:T(8,128)S(1)} copy-done((f32[12,2048]{1,0:T(8,128)S(1)}, f32[12,2048]{1,0:T(8,128)}, u32[]{:S(2)}) %copy-start.1) | copy-done | bytes 98328
  2.7 54.2 %shard_map.50 = (f32[1,512]{1,0:T(1,128)S(1)}, f32[1,512]{1,0:T(1,128)S(1)}) custom-call(f32[12,8,2048]{2,1,0:T(8,128)S(1)} %bitcast.2, f32[12,2048]{1,0:T(8,128)S(1)} %copy-done.1, bf16[12,512,2048]{2,1,0:T(8,128)(2,1)} %bitcast.3), custom_call_target="tpu_custom_call" | custom-call | tf_op jit(solution)/shard_map/pallas_call | solution.py:407
  56.9 0.6 copy.7
  57.5 0.6 copy.8
Async XLA Ops:
  0.6 1.1 %copy-start = (f32[8,12,2048]{2,0,1:T(8,128)S(1)}, f32[8,12,2048]{2,0,1:T(8,128)}, u32[]{:S(2)}) copy-start(f32[8,12,2048]{2,0,1:T(8,128)} %param.3) | copy-start | bytes 2359300
  1.8 0.9 %copy-start.1 = (f32[12,2048]{1,0:T(8,128)S(1)}, f32[12,2048]{1,0:T(8,128)}, u32[]{:S(2)}) copy-start(f32[12,2048]{1,0:T(8,128)} %pot.1) | copy-start | bytes 294916

commit v2 on v1

--- a/solution.py
+++ b/solution.py
@@ -25,6 +25,8 @@
 EXT = 384
 GROUP = 4
 DOM = 32
+AROUND = 1
+ORDER = (2, 3, 1, 4, 0, 5)
 CELLS = 786432
 
 
@@ -79,12 +81,12 @@
 
 
 def kernel(
-    orb_hbm, pot, sub_hbm, corr, proj,
-    orbs, own16, left16, right16, first, second, fleft, fright, rows16, pots, ext, w,
-    sub, even, odd, squares, msg, got,
-    s_loc, s_sub, s_toright, s_toleft, r_left, r_right, s_pot, r_pot,
+    orb_hbm, pot_hbm, sub_hbm, corr, proj,
+    pot, orbs, own16, left16, right16, first, second, applied, fleft, fright, rows16, relay, pots, ext, w,
+    sub, even, odd, msg, got,
+    s_pots, s_loc, s_sub, s_toright, s_toleft, r_left, r_right, s_pot, r_pot,
     s_fright, s_fleft, r_fleft, r_fright,
-    s_z, r_z, s_c, r_c, s_f, r_f, s_all, r_all,
+    s_z, r_z, s_c, r_c, s_f, r_f, s_relay, r_relay, s_all, r_all,
 ):
     d = lax.axis_index("dom")
     b = lax.axis_index("orb")
@@ -93,8 +95,15 @@
     b_z = lax.rem(b + 2, 4)
     b_c = b + 1 - 2 * lax.rem(b, 2)
     b_zc = lax.rem(b_c + 2, 4)
+    x = lax.rem(d, 4)
+    mate = d + 1 - 2 * lax.rem(x, 2)
+    edge = (x == 0) | (x == 3)
 
     barrier = pltpu.get_barrier_semaphore()
+    load = pltpu.make_async_copy(orb_hbm, orbs.at[pl.ds(12, 12)], s_loc)
+    load.start()
+    load_pot = pltpu.make_async_copy(pot_hbm, pot, s_pots)
+    load_pot.start()
 
     def greet(k, carry):
         pl.semaphore_signal(
@@ -103,11 +112,8 @@
         return carry
 
     lax.fori_loop(1, DOM, greet, 0)
-    for peer in (b_z, b_c, b_zc):
-        pl.semaphore_signal(barrier, inc=1, device_id=(d, peer), device_id_type=MESH)
-
-    load = pltpu.make_async_copy(orb_hbm, orbs.at[pl.ds(12, 12)], s_loc)
-    load.start()
+    for peer in ((d, b_z), (d, b_c), (d, b_zc), (mate, b_z)):
+        pl.semaphore_signal(barrier, inc=1, device_id=peer, device_id_type=MESH)
 
     def load_sub(p):
         return pltpu.make_async_copy(sub_hbm.at[p], sub.at[p], s_sub.at[p])
@@ -118,6 +124,9 @@
 
     lax.fori_loop(0, 12, start_sub, 0)
     w[...] = z_matrix()
+    second[pl.ds(0, 6)] = jnp.zeros((6, 8, PLANE), F32)
+    second[pl.ds(18, 6)] = jnp.zeros((6, 8, PLANE), F32)
+    load_pot.wait()
     for p in range(12):
         pots[6 + p] = pot[p : p + 1, :]
     load.wait()
@@ -147,7 +156,7 @@
         pots.at[pl.ds(6, 6)], pots.at[pl.ds(18, 6)], s_pot.at[1], r_pot.at[1], left
     )
 
-    pl.semaphore_wait(barrier, DOM - 1 + 3)
+    pl.semaphore_wait(barrier, DOM - 1 + 4)
 
     def send_orbs(j, carry):
         orb_right(5 - j).start()
@@ -222,6 +231,16 @@
         n = a * 6 + q
         return remote(
             rows16.at[a, b_zc, q], rows16.at[a, b_zc, q], s_f.at[n], r_f.at[n], (d, b_c)
+        )
+
+    def to_mate(q):
+        return remote(
+            rows16.at[0, b, q], relay.at[q], s_z.at[q], r_relay.at[q], (mate, b_z)
+        )
+
+    def from_mate(q):
+        return remote(
+            relay.at[q], rows16.at[0, b_z, q], s_relay.at[q], r_z.at[q], (mate, b)
         )
 
     def filt_right(j):
@@ -250,8 +269,18 @@
         rows16[0, b, 3 + s] = jnp.concatenate(out[2:], axis=0).astype(BF)
         filt_left(2 - s).start()
         filt_right(s).start()
-        to_z(0, 2 - s).start()
-        to_z(0, 3 + s).start()
+        around = edge & (s < AROUND)
+
+        @pl.when(around)
+        def _():
+            to_mate(2 - s).start()
+            to_mate(3 + s).start()
+
+        @pl.when(jnp.logical_not(around))
+        def _():
+            to_z(0, 2 - s).start()
+            to_z(0, 3 + s).start()
+
         to_c(0, 2 - s).start()
         to_c(0, 3 + s).start()
         return carry
@@ -265,41 +294,57 @@
         forward(0, 3 + s).start()
         return carry
 
-    lax.fori_loop(0, 2, pass_on, 0)
-
-    def take_filt(j, carry):
-        filt_right(j).wait_recv()
-        widen(fleft, j, second, 2 * j)
-        filt_left(2 - j).wait_recv()
-        widen(fright, 2 - j, second, 18 + 2 * (2 - j))
-        return carry
-
-    lax.fori_loop(0, 3, take_filt, 0)
-
-    def last(g, carry):
+    def local(g, carry):
         planes = [g * GROUP + j for j in range(GROUP)]
         _, hs = hamiltonian(
             second, [p + 6 for p in planes], [pots[p + 6] for p in planes], w, ext
         )
-        rows16[1, b, 2 * g] = jnp.concatenate(hs[:2], axis=0).astype(BF)
-        rows16[1, b, 2 * g + 1] = jnp.concatenate(hs[2:], axis=0).astype(BF)
-        for q in (2 * g, 2 * g + 1):
-            to_z(1, q).start()
-            to_c(1, q).start()
-        return carry
-
-    lax.fori_loop(0, 3, last, 0)
+        for p, h in zip(planes, hs):
+            applied[p] = h
+        return carry
+
+    lax.fori_loop(0, 3, local, 0)
+
+    def add_halo(j):
+        filt_right(j).wait_recv()
+        filt_left(2 - j).wait_recv()
+        from_left = fleft[j].astype(F32)
+        from_right = fright[2 - j].astype(F32)
+        near, far = 5 - 2 * j, 6 - 2 * j
+        for p in range(7 - near):
+            low = A[near + p] * from_left[8:]
+            high = A[near + p] * from_right[:8]
+            if p <= 6 - far:
+                low = low + A[far + p] * from_left[:8]
+                high = high + A[far + p] * from_right[8:]
+            applied[p] += low
+            applied[11 - p] += high
+
+    @pl.when(jnp.logical_not(edge))
+    def _():
+        for q in ORDER[: 2 * AROUND]:
+            to_mate(q).wait_recv()
+            from_mate(q).start()
+
+    add_halo(0)
+    add_halo(1)
+    pass_on(0, 0)
+    pass_on(1, 0)
+    add_halo(2)
+    for q in ORDER:
+        rows16[1, b, q] = jnp.concatenate([applied[2 * q], applied[2 * q + 1]], axis=0).astype(BF)
+        to_z(1, q).start()
+        to_c(1, q).start()
     pass_on(2, 0)
 
     even[...] = jnp.zeros_like(even)
     odd[...] = jnp.zeros_like(odd)
-    squares[...] = jnp.zeros_like(squares)
 
     def come_on(q):
         come_z(1, q).wait_recv()
         forward(1, q).start()
 
-    def gram(q):
+    def gram(q, total):
         for a in range(2):
             come_c(a, q).wait_recv()
             come_f(a, q).wait_recv()
@@ -311,55 +356,42 @@
         nt = (((1,), (1,)), ((), ()))
         even[...] += lax.dot_general(sub[2 * q], rows, nt, preferred_element_type=F32)
         odd[...] += lax.dot_general(sub[2 * q + 1], rows, nt, preferred_element_type=F32)
-        total = squares[...]
         for c in range(16):
-            x = filt[:, c * 128 : (c + 1) * 128].astype(F32)
-            total = total + x * x
-        squares[...] = total
-
-    come_on(0)
-
-    def step(q, carry):
-        come_on(q + 1)
-        gram(q)
-        return carry
-
-    lax.fori_loop(0, 5, step, 0)
-    gram(5)
+            v = filt[:, c * 128 : (c + 1) * 128].astype(F32)
+            total = total + v * v
+        return total
+
+    def step(s, total):
+        q = 2 - s // 2 + lax.rem(s, 2) * (2 * (s // 2) + 1)
+        after = s + 1
+        come_on(2 - after // 2 + lax.rem(after, 2) * (2 * (after // 2) + 1))
+        return gram(q, total)
+
+    come_on(2)
+    squares = lax.fori_loop(0, 5, step, jnp.zeros((64, 128), F32))
+    squares = gram(5, squares)
 
     from_even = even[...].T
     from_odd = odd[...].T
-    sq = squares[...]
     for o in range(4):
         for a in range(2):
             at = a * 64 + o * 16
             block = from_even[at : at + 8] + from_odd[at + 8 : at + 16]
             for c in range(4):
-                msg[pl.ds(o * 128 + a * 4 + c, 8, stride=16), :] = block[
-                    :, c * 128 : (c + 1) * 128
-                ]
-        msg[pl.ds(o * 128 + 8, 8, stride=16), :] = sq[o * 16 : o * 16 + 8] + sq[o * 16 + 8 : o * 16 + 16]
+                msg[pl.ds(o * 8, 8), a * 4 + c, :] = block[:, c * 128 : (c + 1) * 128]
+        msg[pl.ds(o * 8, 8), 8, :] = squares[o * 16 : o * 16 + 8] + squares[o * 16 + 8 : o * 16 + 16]
 
     def to_all(k):
         t = lax.rem(d + k, DOM)
-        return remote(
-            msg.at[pl.ds(t * 16, 16)], got.at[pl.ds(d * 16, 16)],
-            s_all.at[k - 1], r_all.at[k - 1], (t, b),
-        )
+        return remote(msg.at[t], got.at[d], s_all.at[k], r_all.at[k], (t, b))
 
     def from_all(k):
         t = lax.rem(d + DOM - k, DOM)
-        return remote(
-            msg.at[pl.ds(t * 16, 16)], got.at[pl.ds(t * 16, 16)],
-            s_all.at[k - 1], r_all.at[k - 1], (t, b),
-        )
-
-    def send_all(k, carry):
+        return remote(msg.at[t], got.at[t], s_all.at[k], r_all.at[k], (t, b))
+
+    for k in sorted(range(1, DOM), key=lambda k: abs(k - DOM // 2)):
         to_all(k).start()
-        return carry
-
-    lax.fori_loop(1, DOM, send_all, 0)
-    got[pl.ds(d * 16, 16), :] = msg[pl.ds(d * 16, 16), :]
+    got[d] = msg[d]
 
     def wait_sends(j, carry):
         orb_right(j).wait_send()
@@ -378,28 +410,26 @@
         return carry
 
     lax.fori_loop(0, 3, wait_filt, 0)
+    @pl.when(jnp.logical_not(edge))
+    def _():
+        for q in ORDER[: 2 * AROUND]:
+            from_mate(q).wait_send()
+
     pot_right.wait_send()
     pot_left.wait_send()
 
-    def wait_all(k, carry):
+    for k in range(1, DOM):
+        to_all(k).wait_send()
+    for k in range(1, DOM):
         from_all(k).wait_recv()
-        return carry
-
-    lax.fori_loop(1, DOM, wait_all, 0)
-    total = got[pl.ds(0, 16), :]
+    total = got[0]
     for t in range(1, DOM):
-        total = total + got[pl.ds(t * 16, 16), :]
-    scale = jnp.sqrt(jnp.sum(total[8:9, :], axis=1, keepdims=True) / CELLS + 1e-06)
+        total = total + got[t]
+    scale = jnp.sqrt(jnp.sum(total[8:], axis=1, keepdims=True) / CELLS + 1e-06)
     total = total[:8] / scale
     for c in range(4):
         corr[:, c * 128 : (c + 1) * 128] = total[c : c + 1]
         proj[:, c * 128 : (c + 1) * 128] = total[4 + c : 5 + c]
-
-    def wait_sent(k, carry):
-        to_all(k).wait_send()
-        return carry
-
-    lax.fori_loop(1, DOM, wait_sent, 0)
 
 
 def shards(orbitals, potential, subspace):
@@ -408,38 +438,40 @@
         kernel,
         out_shape=[jax.ShapeDtypeStruct((1, 512), F32)] * 2,
         in_specs=[
-            pl.BlockSpec(memory_space=pl.ANY),
-            pl.BlockSpec(memory_space=pltpu.VMEM),
-            pl.BlockSpec(memory_space=pl.ANY),
+            pl.BlockSpec(memory_space=pltpu.HBM),
+            pl.BlockSpec(memory_space=pltpu.HBM),
+            pl.BlockSpec(memory_space=pltpu.HBM),
         ],
         out_specs=[pl.BlockSpec(memory_space=pltpu.VMEM)] * 2,
         scratch_shapes=[
+            pltpu.VMEM((12, PLANE), F32),
             pltpu.VMEM((36, 8, PLANE), F32),
             pltpu.VMEM((6, 16, PLANE), BF),
             pltpu.VMEM((6, 16, PLANE), BF),
             pltpu.VMEM((6, 16, PLANE), BF),
             pltpu.VMEM((24, 8, PLANE), F32),
             pltpu.VMEM((24, 8, PLANE), F32),
+            pltpu.VMEM((12, 8, PLANE), F32),
             pltpu.VMEM((3, 16, PLANE), BF),
             pltpu.VMEM((3, 16, PLANE), BF),
             pltpu.VMEM((2, 4, 6, 16, PLANE), BF),
+            pltpu.VMEM((6, 16, PLANE), BF),
             pltpu.VMEM((24, 1, PLANE), F32),
             pltpu.VMEM((GROUP, 2, 8, PLANE + 2 * EXT), F32),
             pltpu.VMEM((256, 256), BF),
             pltpu.VMEM((12, 512, PLANE), BF),
             pltpu.VMEM((512, 128), F32),
             pltpu.VMEM((512, 128), F32),
-            pltpu.VMEM((64, 128), F32),
-            pltpu.VMEM((DOM * 16, 128), F32),
-            pltpu.VMEM((DOM * 16, 128), F32),
-            dma(()), dma((12,)),
+            pltpu.VMEM((DOM, 9, 128), F32),
+            pltpu.VMEM((DOM, 9, 128), F32),
+            dma(()), dma(()), dma((12,)),
             dma((6,)), dma((6,)), dma((6,)), dma((6,)), dma((2,)), dma((2,)),
             dma((3,)), dma((3,)), dma((3,)), dma((3,)),
             dma((12,)), dma((12,)), dma((12,)), dma((12,)), dma((12,)), dma((12,)),
-            dma((DOM - 1,)), dma((DOM - 1,)),
+            dma((6,)), dma((6,)), dma((DOM,)), dma((DOM,)),
         ],
         compiler_params=pltpu.CompilerParams(
-            collective_id=0, has_side_effects=True, vmem_limit_bytes=48 * 2**20
+            collective_id=0, has_side_effects=True, vmem_limit_bytes=64 * 2**20 - 10400 * 1024
         ),
     )(orbitals.transpose(1, 0, 2), potential, subspace.transpose(1, 0, 2))
 

time: 58.3 us -> 54.9 us (0.942)
  local copies, waits for them, and re-layouts: 3.19 us -> 1.16 us
  Pallas kernels: 54.2 us -> 52.8 us
    unnamed x6 -> x2, local copies, waits for them, and re-layouts: 3.19 us -> 1.16 us
    pallas_call x1, Pallas kernels: 54.2 us -> 52.8 us  [shards(): pl.pallas_call(kernel, out_shape=[jax.ShapeDtypeStruct((1, 512), F32)] *...]
where the time goes in v2:
time: 54.9 us; the launch traced here: 54.6 us
  Pallas kernels  52.8 us (96%)
  local copies, waits for them, and re-layouts  1.16 us (2%)
  between operations  0.64 us (1%)
    pallas_call x1, Pallas kernels, shards(): pl.pallas_call(kernel, out_shape=[jax.ShapeDtypeStruct((1, 512), F32)] *...  52.8 us
    unnamed x2, local copies, waits for them, and re-layouts  1.16 us

profile of v2, /device:TPU:0, one launch (start us, length us, event | category | flops | bytes accessed | tf_op | source)
XLA Modules:
  0.0 54.6 jit_solution(610818548457173402)
XLA Ops:
  0.6 52.8 %shard_map.50 = (f32[1,512]{1,0:T(1,128)S(1)}, f32[1,512]{1,0:T(1,128)S(1)}) custom-call(f32[12,8,2048]{2,1,0:T(8,128)} %bitcast.3, f32[12,2048]{1,0:T(8,128)} %pot_hbm.1, bf16[12,512,2048]{2,1,0:T(8,128)(2,1)} %bitcast.2), custom_call_target="tpu_custom_call" | custom-call | tf_op jit(solution)/shard_map/pallas_call | solution.py:437
  53.4 0.6 %copy.7 = f32[1,512]{1,0:T(1,128)} copy(f32[1,512]{1,0:T(1,128)S(1)} %get-tuple-element.4) | data formatting | bytes 4096
  54.0 0.6 %copy.8 = f32[1,512]{1,0:T(1,128)} copy(f32[1,512]{1,0:T(1,128)S(1)} %get-tuple-element.5) | data formatting | bytes 4096

commit v3 on v2

--- a/solution.py
+++ b/solution.py
@@ -81,10 +81,10 @@
 
 
 def kernel(
-    orb_hbm, pot_hbm, sub_hbm, corr, proj,
+    orb_hbm, pot_hbm, sub_hbm, both,
     pot, orbs, own16, left16, right16, first, second, applied, fleft, fright, rows16, relay, pots, ext, w,
     sub, even, odd, msg, got,
-    s_pots, s_loc, s_sub, s_toright, s_toleft, r_left, r_right, s_pot, r_pot,
+    s_pots, s_loc, s_sub, s_toright, s_toleft, r_left, r_right, s_pot, r_pot, s_share, r_share,
     s_fright, s_fleft, r_fleft, r_fright,
     s_z, r_z, s_c, r_c, s_f, r_f, s_relay, r_relay, s_all, r_all,
 ):
@@ -123,9 +123,6 @@
         return carry
 
     lax.fori_loop(0, 12, start_sub, 0)
-    w[...] = z_matrix()
-    second[pl.ds(0, 6)] = jnp.zeros((6, 8, PLANE), F32)
-    second[pl.ds(18, 6)] = jnp.zeros((6, 8, PLANE), F32)
     load_pot.wait()
     for p in range(12):
         pots[6 + p] = pot[p : p + 1, :]
@@ -149,12 +146,20 @@
     def orb_left(q):
         return remote(own16.at[q], right16.at[q], s_toleft.at[q], r_right.at[q], left)
 
-    pot_right = remote(
-        pots.at[pl.ds(12, 6)], pots.at[pl.ds(0, 6)], s_pot.at[0], r_pot.at[0], right
-    )
-    pot_left = remote(
-        pots.at[pl.ds(6, 6)], pots.at[pl.ds(18, 6)], s_pot.at[1], r_pot.at[1], left
-    )
+    def half(start, o):
+        at = pl.multiple_of(lax.rem(o, 2) * 1024, 1024)
+        return pots.at[pl.ds(start, 6), :, pl.ds(at, 1024)]
+
+    pot_right = remote(half(12, b), half(0, b), s_pot.at[0], r_pot.at[0], right)
+    pot_left = remote(half(6, b), half(18, b), s_pot.at[1], r_pot.at[1], left)
+
+    def share(side):
+        mine = half(18 * side, b)
+        return remote(mine, mine, s_share.at[side], r_share.at[side], (d, b_c))
+
+    def shared(side):
+        other = half(18 * side, b_c)
+        return remote(other, other, s_share.at[side], r_share.at[side], (d, b_c))
 
     pl.semaphore_wait(barrier, DOM - 1 + 4)
 
@@ -163,10 +168,9 @@
         orb_left(j).start()
         return carry
 
-    lax.fori_loop(0, 3, send_orbs, 0)
     pot_right.start()
     pot_left.start()
-    lax.fori_loop(3, 6, send_orbs, 0)
+    lax.fori_loop(0, 6, send_orbs, 0)
 
     def widen(src, q, dst, at):
         both = src[q].astype(F32)
@@ -180,6 +184,13 @@
         widen(right16, j, orbs, 24 + 2 * j)
         return carry
 
+    w[...] = z_matrix()
+    second[pl.ds(0, 6)] = jnp.zeros((6, 8, PLANE), F32)
+    second[pl.ds(18, 6)] = jnp.zeros((6, 8, PLANE), F32)
+    pot_right.wait_recv()
+    share(0).start()
+    pot_left.wait_recv()
+    share(1).start()
     lax.fori_loop(0, 3, take_orbs, 0)
 
     def first_of(planes):
@@ -194,8 +205,8 @@
         return carry
 
     lax.fori_loop(0, 3, inner, 0)
-    pot_right.wait_recv()
-    pot_left.wait_recv()
+    shared(0).wait_recv()
+    shared(1).wait_recv()
 
     def to_z(a, q):
         n = a * 6 + q
@@ -417,6 +428,8 @@
 
     pot_right.wait_send()
     pot_left.wait_send()
+    share(0).wait_send()
+    share(1).wait_send()
 
     for k in range(1, DOM):
         to_all(k).wait_send()
@@ -428,21 +441,21 @@
     scale = jnp.sqrt(jnp.sum(total[8:], axis=1, keepdims=True) / CELLS + 1e-06)
     total = total[:8] / scale
     for c in range(4):
-        corr[:, c * 128 : (c + 1) * 128] = total[c : c + 1]
-        proj[:, c * 128 : (c + 1) * 128] = total[4 + c : 5 + c]
+        both[0:1, c * 128 : (c + 1) * 128] = total[c : c + 1]
+        both[1:2, c * 128 : (c + 1) * 128] = total[4 + c : 5 + c]
 
 
 def shards(orbitals, potential, subspace):
     dma = pltpu.SemaphoreType.DMA
-    return pl.pallas_call(
+    both = pl.pallas_call(
         kernel,
-        out_shape=[jax.ShapeDtypeStruct((1, 512), F32)] * 2,
+        out_shape=jax.ShapeDtypeStruct((2, 512), F32),
         in_specs=[
             pl.BlockSpec(memory_space=pltpu.HBM),
             pl.BlockSpec(memory_space=pltpu.HBM),
             pl.BlockSpec(memory_space=pltpu.HBM),
         ],
-        out_specs=[pl.BlockSpec(memory_space=pltpu.VMEM)] * 2,
+        out_specs=pl.BlockSpec(memory_space=pltpu.VMEM),
         scratch_shapes=[
             pltpu.VMEM((12, PLANE), F32),
             pltpu.VMEM((36, 8, PLANE), F32),
@@ -465,7 +478,7 @@
             pltpu.VMEM((DOM, 9, 128), F32),
             pltpu.VMEM((DOM, 9, 128), F32),
             dma(()), dma(()), dma((12,)),
-            dma((6,)), dma((6,)), dma((6,)), dma((6,)), dma((2,)), dma((2,)),
+            dma((6,)), dma((6,)), dma((6,)), dma((6,)), dma((2,)), dma((2,)), dma((2,)), dma((2,)),
             dma((3,)), dma((3,)), dma((3,)), dma((3,)),
             dma((12,)), dma((12,)), dma((12,)), dma((12,)), dma((12,)), dma((12,)),
             dma((6,)), dma((6,)), dma((DOM,)), dma((DOM,)),
@@ -474,6 +487,7 @@
             collective_id=0, has_side_effects=True, vmem_limit_bytes=64 * 2**20 - 10400 * 1024
         ),
     )(orbitals.transpose(1, 0, 2), potential, subspace.transpose(1, 0, 2))
+    return both[0:1], both[1:2]
 
 
 def solution(mesh):

time: 54.9 us -> 53.9 us (0.982)
  local copies, waits for them, and re-layouts: 1.16 us -> 0.59 us
    unnamed x2 -> x0, local copies, waits for them, and re-layouts: 1.16 us -> none
    slice x0 -> x1, local copies, waits for them, and re-layouts: none -> 0.59 us  [shards(): return (both[0:1], both[1:2])]
where the time goes in v3:
time: 53.9 us; the launch traced here: 53.5 us
  Pallas kernels  52.3 us (97%)
  between operations  0.64 us (1%)
  local copies, waits for them, and re-layouts  0.59 us (1%)
    pallas_call x1, Pallas kernels, shards(): pl.pallas_call(kernel, out_shape=jax.ShapeDtypeStruct((2, 512), F32), in_...  52.3 us

profile of v3, /device:TPU:0, one launch (start us, length us, event | category | flops | bytes accessed | tf_op | source)
XLA Modules:
  0.0 53.5 jit_solution(12618029706471792080)
XLA Ops:
  0.6 52.3 %shard_map.50 = f32[2,512]{1,0:T(2,128)S(1)} custom-call(f32[12,8,2048]{2,1,0:T(8,128)} %bitcast.3, f32[12,2048]{1,0:T(8,128)} %pot_hbm.1, bf16[12,512,2048]{2,1,0:T(8,128)(2,1)} %bitcast.2), custom_call_target="tpu_custom_call" | custom-call | tf_op jit(solution)/shard_map/pallas_call | solution.py:450
  52.9 0.6 %fusion = (f32[1,512]{1,0:T(1,128)}, f32[1,512]{1,0:T(1,128)}) fusion(f32[2,512]{1,0:T(2,128)S(1)} %shard_map.50), kind=kLoop, calls=%fused_computation | loop fusion | bytes 8192 | tf_op jit(solution)/shard_map/slice | solution.py:490

commit v4 on v3

--- a/solution.py
+++ b/solution.py
@@ -84,7 +84,7 @@
     orb_hbm, pot_hbm, sub_hbm, both,
     pot, orbs, own16, left16, right16, first, second, applied, fleft, fright, rows16, relay, pots, ext, w,
     sub, even, odd, msg, got,
-    s_pots, s_loc, s_sub, s_toright, s_toleft, r_left, r_right, s_pot, r_pot, s_share, r_share,
+    row_in, plane_in, s_pots, s_loc, s_sub, s_toright, s_toleft, r_left, r_right, s_pot, r_pot, s_share, r_share,
     s_fright, s_fleft, r_fleft, r_fright,
     s_z, r_z, s_c, r_c, s_f, r_f, s_relay, r_relay, s_all, r_all,
 ):
@@ -105,14 +105,12 @@
     load_pot = pltpu.make_async_copy(pot_hbm, pot, s_pots)
     load_pot.start()
 
-    def greet(k, carry):
-        pl.semaphore_signal(
-            barrier, inc=1, device_id=(lax.rem(d + k, DOM), b), device_id_type=MESH
-        )
-        return carry
-
-    lax.fori_loop(1, DOM, greet, 0)
-    for peer in ((d, b_z), (d, b_c), (d, b_zc), (mate, b_z)):
+    beyond = d + 4 - 8 * lax.rem(d // 4, 2)
+    same_y = [d - x + lax.rem(x + k, 4) for k in range(1, 4)]
+    across_y = [lax.rem(d + 8 * k, DOM) for k in range(1, 4)]
+    peers_in = [right, left, (d, b_z), (d, b_c), (d, b_zc), (mate, b_z)]
+    peers_in += [(t, b) for t in [*same_y, *across_y, beyond]]
+    for peer in peers_in:
         pl.semaphore_signal(barrier, inc=1, device_id=peer, device_id_type=MESH)
 
     def load_sub(p):
@@ -161,7 +159,7 @@
         other = half(18 * side, b_c)
         return remote(other, other, s_share.at[side], r_share.at[side], (d, b_c))
 
-    pl.semaphore_wait(barrier, DOM - 1 + 4)
+    pl.semaphore_wait(barrier, len(peers_in))
 
     def send_orbs(j, carry):
         orb_right(5 - j).start()
@@ -171,6 +169,9 @@
     pot_right.start()
     pot_left.start()
     lax.fori_loop(0, 6, send_orbs, 0)
+
+    for t in across_y:
+        pl.semaphore_signal(row_in, inc=1, device_id=(t, b), device_id_type=MESH)
 
     def widen(src, q, dst, at):
         both = src[q].astype(F32)
@@ -207,6 +208,8 @@
     lax.fori_loop(0, 3, inner, 0)
     shared(0).wait_recv()
     shared(1).wait_recv()
+    pl.semaphore_wait(row_in, len(across_y))
+    pl.semaphore_signal(plane_in, inc=1, device_id=(beyond, b), device_id_type=MESH)
 
     def to_z(a, q):
         n = a * 6 + q
@@ -348,6 +351,7 @@
         to_c(1, q).start()
     pass_on(2, 0)
 
+    pl.semaphore_wait(plane_in, 1)
     even[...] = jnp.zeros_like(even)
     odd[...] = jnp.zeros_like(odd)
 
@@ -400,7 +404,7 @@
         t = lax.rem(d + DOM - k, DOM)
         return remote(msg.at[t], got.at[t], s_all.at[k], r_all.at[k], (t, b))
 
-    for k in sorted(range(1, DOM), key=lambda k: abs(k - DOM // 2)):
+    for k in range(1, DOM):
         to_all(k).start()
     got[d] = msg[d]
 
@@ -477,6 +481,7 @@
             pltpu.VMEM((512, 128), F32),
             pltpu.VMEM((DOM, 9, 128), F32),
             pltpu.VMEM((DOM, 9, 128), F32),
+            pltpu.SemaphoreType.REGULAR, pltpu.SemaphoreType.REGULAR,
             dma(()), dma(()), dma((12,)),
             dma((6,)), dma((6,)), dma((6,)), dma((6,)), dma((2,)), dma((2,)), dma((2,)), dma((2,)),
             dma((3,)), dma((3,)), dma((3,)), dma((3,)),

time: 53.9 us -> 52.8 us (0.980)
  Pallas kernels: 52.3 us -> 51.2 us
    pallas_call x1, Pallas kernels: 52.3 us -> 51.2 us  [shards(): pl.pallas_call(kernel, out_shape=jax.ShapeDtypeStruct((2, 512), F32), in_...]
where the time goes in v4:
time: 52.8 us; the launch traced here: 52.5 us
  Pallas kernels  51.2 us (97%)
  between operations  0.64 us (1%)
  local copies, waits for them, and re-layouts  0.59 us (1%)
    pallas_call x1, Pallas kernels, shards(): pl.pallas_call(kernel, out_shape=jax.ShapeDtypeStruct((2, 512), F32), in_...  51.2 us

profile of v4, /device:TPU:0, one launch (start us, length us, event | category | flops | bytes accessed | tf_op | source)
XLA Modules:
  0.0 52.5 jit_solution(11846811083706526954)
XLA Ops:
  0.6 51.2 %shard_map.50 = f32[2,512]{1,0:T(2,128)S(1)} custom-call(f32[12,8,2048]{2,1,0:T(8,128)} %bitcast.3, f32[12,2048]{1,0:T(8,128)} %pot_hbm.1, bf16[12,512,2048]{2,1,0:T(8,128)(2,1)} %bitcast.2), custom_call_target="tpu_custom_call" | custom-call | tf_op jit(solution)/shard_map/pallas_call | solution.py:454
  51.9 0.6 %fusion = (f32[1,512]{1,0:T(1,128)}, f32[1,512]{1,0:T(1,128)}) fusion(f32[2,512]{1,0:T(2,128)S(1)} %shard_map.50), kind=kLoop, calls=%fused_computation | loop fusion | bytes 8192 | tf_op jit(solution)/shard_map/slice | solution.py:495

commit v5 on v4

--- a/solution.py
+++ b/solution.py
@@ -288,7 +288,7 @@
         @pl.when(around)
         def _():
             to_mate(2 - s).start()
-            to_mate(3 + s).start()
+            to_z(0, 3 + s).start()
 
         @pl.when(jnp.logical_not(around))
         def _():
@@ -325,7 +325,7 @@
         from_left = fleft[j].astype(F32)
         from_right = fright[2 - j].astype(F32)
         near, far = 5 - 2 * j, 6 - 2 * j
-        for p in range(7 - near):
+        for p in reversed(range(7 - near)):
             low = A[near + p] * from_left[8:]
             high = A[near + p] * from_right[:8]
             if p <= 6 - far:
@@ -336,7 +336,7 @@
 
     @pl.when(jnp.logical_not(edge))
     def _():
-        for q in ORDER[: 2 * AROUND]:
+        for q in ORDER[:AROUND]:
             to_mate(q).wait_recv()
             from_mate(q).start()
 
@@ -386,12 +386,11 @@
     squares = lax.fori_loop(0, 5, step, jnp.zeros((64, 128), F32))
     squares = gram(5, squares)
 
-    from_even = even[...].T
-    from_odd = odd[...].T
+    by_row = (even[...] + pltpu.roll(odd[...], 120, 1)).T
     for o in range(4):
         for a in range(2):
             at = a * 64 + o * 16
-            block = from_even[at : at + 8] + from_odd[at + 8 : at + 16]
+            block = by_row[at : at + 8]
             for c in range(4):
                 msg[pl.ds(o * 8, 8), a * 4 + c, :] = block[:, c * 128 : (c + 1) * 128]
         msg[pl.ds(o * 8, 8), 8, :] = squares[o * 16 : o * 16 + 8] + squares[o * 16 + 8 : o * 16 + 16]
@@ -427,7 +426,7 @@
     lax.fori_loop(0, 3, wait_filt, 0)
     @pl.when(jnp.logical_not(edge))
     def _():
-        for q in ORDER[: 2 * AROUND]:
+        for q in ORDER[:AROUND]:
             from_mate(q).wait_send()
 
     pot_right.wait_send()

time: 52.8 us -> 52.3 us (level)
  no operation moved by 1% of the time
where the time goes in v5:
time: 52.3 us; the launch traced here: 52.1 us
  Pallas kernels  50.9 us (97%)
  between operations  0.64 us (1%)
  local copies, waits for them, and re-layouts  0.59 us (1%)
    pallas_call x1, Pallas kernels, shards(): pl.pallas_call(kernel, out_shape=jax.ShapeDtypeStruct((2, 512), F32), in_...  50.9 us

profile of v5, /device:TPU:0, one launch (start us, length us, event | category | flops | bytes accessed | tf_op | source)
XLA Modules:
  0.0 52.1 jit_solution(1953248559577590177)
XLA Ops:
  0.6 50.9 %shard_map.50 = f32[2,512]{1,0:T(2,128)S(1)} custom-call(f32[12,8,2048]{2,1,0:T(8,128)} %bitcast.3, f32[12,2048]{1,0:T(8,128)} %pot_hbm.1, bf16[12,512,2048]{2,1,0:T(8,128)(2,1)} %bitcast.2), custom_call_target="tpu_custom_call" | custom-call | tf_op jit(solution)/shard_map/pallas_call | solution.py:453
  51.5 0.6 %fusion = (f32[1,512]{1,0:T(1,128)}, f32[1,512]{1,0:T(1,128)}) fusion(f32[2,512]{1,0:T(2,128)S(1)} %shard_map.50), kind=kLoop, calls=%fused_computation | loop fusion | bytes 8192 | tf_op jit(solution)/shard_map/slice | solution.py:494

commit v6 on v5

--- a/solution.py
+++ b/solution.py
@@ -120,7 +120,6 @@
         load_sub(p).start()
         return carry
 
-    lax.fori_loop(0, 12, start_sub, 0)
     load_pot.wait()
     for p in range(12):
         pots[6 + p] = pot[p : p + 1, :]
@@ -185,6 +184,7 @@
         widen(right16, j, orbs, 24 + 2 * j)
         return carry
 
+    lax.fori_loop(0, 12, start_sub, 0)
     w[...] = z_matrix()
     second[pl.ds(0, 6)] = jnp.zeros((6, 8, PLANE), F32)
     second[pl.ds(18, 6)] = jnp.zeros((6, 8, PLANE), F32)

time: 52.3 us -> 52.3 us (level)
  no operation moved by 1% of the time
where the time goes in v6:
time: 52.3 us; the launch traced here: 52.1 us
  Pallas kernels  50.9 us (97%)
  between operations  0.64 us (1%)
  local copies, waits for them, and re-layouts  0.59 us (1%)
    pallas_call x1, Pallas kernels, shards(): pl.pallas_call(kernel, out_shape=jax.ShapeDtypeStruct((2, 512), F32), in_...  50.9 us

profile of v6, /device:TPU:0, one launch (start us, length us, event | category | flops | bytes accessed | tf_op | source)
XLA Modules:
  0.0 52.1 jit_solution(11951596213933226256)
XLA Ops:
  0.6 50.9 %shard_map.50 = f32[2,512]{1,0:T(2,128)S(1)} custom-call(f32[12,8,2048]{2,1,0:T(8,128)} %bitcast.3, f32[12,2048]{1,0:T(8,128)} %pot_hbm.1, bf16[12,512,2048]{2,1,0:T(8,128)(2,1)} %bitcast.2), custom_call_target="tpu_custom_call" | custom-call | tf_op jit(solution)/shard_map/pallas_call | solution.py:453
  51.5 0.6 %fusion = (f32[1,512]{1,0:T(1,128)}, f32[1,512]{1,0:T(1,128)}) fusion(f32[2,512]{1,0:T(2,128)S(1)} %shard_map.50), kind=kLoop, calls=%fused_computation | loop fusion | bytes 8192 | tf_op jit(solution)/shard_map/slice | solution.py:494
